TPU v7x, 32 devices: a whole 2x2x4 slice. The times are simulated.
32 devices in a mesh: pat: 2 (over x), gx: 16 (over z, y, core).
Axes of the slice: x: 2, y: 2, z: 4, core: 2. Of those that a mesh axis runs over, the one named last changes fastest.
Arguments:
- pattern_index: int32 [2], P('pat'), may hold values from 0 to 7
- patterns: float32 [8, 128, 1024], P(None, 'gx'), may hold values from -6 to 6
- freq_bins: int32 [16], replicated, may hold values from 0 to 127
- absorption: float32 [128, 1024, 128], P('gx'), may hold values from 0.05 to 0.5
- forward_start: float32 [2, 128, 1024, 128], P('pat', 'gx'), may hold values from -6 to 6
- adjoint_start: float32 [2, 128, 1024, 128], P('pat', 'gx'), may hold values from -6 to 6
- measured: float32 [2, 2, 16, 1024], P('pat', None, None, 'gx'), may hold values from -6 to 6
Outputs:
- gradient: float32 [128, 1024, 128], P('gx', 'pat')
- model: float32 [2, 2, 16, 1024], P('pat', None, None, 'gx')
All inputs are finite; a program needn't handle non-finite values.
Results may differ from a plain program's by a relative error of at most 0.00029.
Values sent between devices are 32-bit elements; how exact they have to be, the bound alone decides.
A program may use at most 128 MiB of HBM per device.

v0:
```python
import functools
import math

import jax
import jax.numpy as jnp
from jax import lax
from jax.experimental import pallas as pl
from jax.experimental.pallas import tpu as pltpu
from jax.sharding import PartitionSpec as P

SWEEPS = 4
EDGE = 8
LANES = 128
MESH = pl.DeviceIdType.MESH


def sweep_weight(sweep):
    return 1.0 / (1.25 + 0.75 * math.cos(math.pi * (2 * sweep + 1) / (2 * SWEEPS)))


def make_tables(freq_bins, positions, total_x):
    phase = freq_bins[:, None] * positions[None, :] % total_x
    angle = 2.0 * math.pi / total_x * phase.astype(jnp.float32)
    return (jnp.cos(angle) / math.sqrt(total_x), jnp.sin(angle) / math.sqrt(total_x))


def chunk_rows(rows):
    tiles = rows // 8
    for size in range(min(tiles, 13), 0, -1):
        if tiles % size == 0:
            return size * 8
    return 8


def solve_kernel(
    count, planes, ny, depth,
    fwd, adj, absorb, fsrc, asrc, out,
    buf, inv, srcs, gsend, grecv,
    load_sems, send_sems, recv_sems, gsend_sems, grecv_sems,
):
    half = ny // 2
    span = half + EDGE
    me = lax.axis_index("gx")
    pat = lax.axis_index("pat")
    last = count - 1
    has_low = jnp.where(me > 0, 1, 0)
    has_high = jnp.where(me < last, 1, 0)

    first_row = (
        pl.multiple_of((1 - pat) * (half - EDGE), 8),
        pl.multiple_of(pat * (half - EDGE), 8),
    )
    skip = (pl.multiple_of((1 - pat) * EDGE, 8), pl.multiple_of(pat * EDGE, 8))

    loads = []
    for part in range(2):
        rows = pl.ds(first_row[part], span)
        inner = (pl.ds(1, planes), pl.ds(8, span))
        group = (
            pltpu.make_async_copy(
                fwd.at[:, rows], buf.at[(part, 0, 0) + inner], load_sems.at[part, 0]
            ),
            pltpu.make_async_copy(
                adj.at[:, rows], buf.at[(part, 1, 0) + inner], load_sems.at[part, 1]
            ),
            pltpu.make_async_copy(absorb.at[:, rows], inv.at[part], load_sems.at[part, 2]),
            pltpu.make_async_copy(fsrc.at[rows], srcs.at[part, 0], load_sems.at[part, 3]),
            pltpu.make_async_copy(asrc.at[rows], srcs.at[part, 1], load_sems.at[part, 4]),
        )
        for copy in group:
            copy.start()
        loads.append(group)

    barrier = pltpu.get_barrier_semaphore()
    pl.semaphore_signal(barrier, inc=1, device_id={"pat": 1 - pat}, device_id_type=MESH)

    @pl.when(me > 0)
    def _():
        pl.semaphore_signal(barrier, inc=1, device_id={"gx": me - 1}, device_id_type=MESH)

    @pl.when(me < last)
    def _():
        pl.semaphore_signal(barrier, inc=1, device_id={"gx": me + 1}, device_id_type=MESH)

    edge_rows = jnp.zeros((8, depth), jnp.float32)

    def clear_edges(i, _):
        part, field, slot, plane = i // (4 * planes), i // (2 * planes) % 2, i // planes % 2, i % planes
        buf[part, field, slot, plane + 1, 0:8] = edge_rows
        buf[part, field, slot, plane + 1, 8 + span : 16 + span] = edge_rows
        return 0

    lax.fori_loop(0, 8 * planes, clear_edges, 0)

    def clear_plane(plane):
        def body(i, _):
            buf[i // 4, i // 2 % 2, i % 2, plane] = jnp.zeros((16 + span, depth), jnp.float32)
            return 0

        lax.fori_loop(0, 8, body, 0)

    @pl.when(me == 0)
    def _():
        clear_plane(0)

    @pl.when(me == last)
    def _():
        clear_plane(planes + 1)

    pl.semaphore_wait(barrier, 1 + has_low + has_high)

    rows_held = pl.ds(8, span)

    def face(part, field, sweep, side):
        slot = sweep % 2
        return pltpu.make_async_remote_copy(
            src_ref=buf.at[part, field, slot, 1 if side == 0 else planes, rows_held],
            dst_ref=buf.at[part, field, slot, planes + 1 if side == 0 else 0, rows_held],
            send_sem=send_sems.at[part, field, sweep, side],
            recv_sem=recv_sems.at[part, field, sweep, side],
            device_id={"gx": me - 1 if side == 0 else me + 1},
            device_id_type=MESH,
        )

    def send_faces(part, field, sweep):
        @pl.when(me > 0)
        def _():
            face(part, field, sweep, 0).start()

        @pl.when(me < last)
        def _():
            face(part, field, sweep, 1).start()

    def wait_sent(part, field, sweep):
        @pl.when(me > 0)
        def _():
            face(part, field, sweep, 0).wait_send()

        @pl.when(me < last)
        def _():
            face(part, field, sweep, 1).wait_send()

    def wait_faces(part, field, sweep):
        @pl.when(me > 0)
        def _():
            face(part, field, sweep, 1).wait_recv()

        @pl.when(me < last)
        def _():
            face(part, field, sweep, 0).wait_recv()

    def invert(part):
        step = chunk_rows(span)

        def body(plane, _):
            for at in range(0, span, step):
                inv[part, plane, at : at + step] = 1.0 / (6.0 + inv[part, plane, at : at + step])
            return 0

        lax.fori_loop(0, planes, body, 0)

    for field in range(2):
        loads[0][field].wait()
        send_faces(0, field, 0)
    for copy in loads[0][2:]:
        copy.wait()
    invert(0)
    for copy in loads[1]:
        copy.wait()
    invert(1)

    step_rows = chunk_rows(span)
    lane = lax.broadcasted_iota(jnp.int32, (step_rows, depth), 1)
    top = lane == 0
    bottom = lane == depth - 1

    def update(part, field, sweep, plane, weight):
        now, later = sweep % 2, (sweep + 1) % 2
        at_now = (part, field, now)
        for at in range(0, span, step_rows):
            here = pl.ds(8 + at, step_rows)
            center = buf[part, field, now, plane, here]
            column = srcs[part, field, pl.ds(at, step_rows)]
            column = pltpu.roll(column, lax.rem(depth + 1 - plane, depth), 1)
            beside = buf[part, field, now, plane - 1, here] + buf[part, field, now, plane + 1, here]
            beside = beside + buf[part, field, now, plane, pl.ds(7 + at, step_rows)]
            beside = beside + buf[part, field, now, plane, pl.ds(9 + at, step_rows)]
            beside = beside + jnp.where(top, column, pltpu.roll(center, 1, 1))
            beside = beside + jnp.where(bottom, 0.0, pltpu.roll(center, depth - 1, 1))
            scale = inv[part, plane - 1, pl.ds(at, step_rows)]
            buf[part, field, later, plane, here] = center + weight * (beside * scale - center)

    def one_step(index, _):
        field = index % 2
        stage = index // 2
        part, sweep = stage // SWEEPS, stage % SWEEPS
        weight = jnp.float32(sweep_weight(0))
        for other in range(1, SWEEPS):
            weight = jnp.where(sweep == other, jnp.float32(sweep_weight(other)), weight)
        wait_faces(part, field, sweep)

        @pl.when(sweep > 0)
        def _():
            wait_sent(part, field, sweep - 1)

        def outer(i, _):
            update(part, field, sweep, 1 + i * (planes - 1), weight)
            return 0

        lax.fori_loop(0, 2, outer, 0)
        coming = stage + 1

        @pl.when(coming < 2 * SWEEPS)
        def _():
            send_faces(coming // SWEEPS, field, coming % SWEEPS)

        def within(plane, _):
            update(part, field, sweep, plane, weight)
            return 0

        lax.fori_loop(2, planes, within, 0)
        return 0

    def terms(part, plane, at, rows):
        where = pl.ds(8 + skip[part] + at, rows)
        slot = SWEEPS % 2
        return -(buf[part, 0, slot, plane + 1, where] * buf[part, 1, slot, plane + 1, where])

    term_rows = chunk_rows(half)

    def swap(plane):
        return pltpu.make_async_remote_copy(
            src_ref=gsend.at[plane],
            dst_ref=grecv.at[plane],
            send_sem=gsend_sems.at[plane],
            recv_sem=grecv_sems.at[plane],
            device_id={"pat": 1 - pat},
            device_id_type=MESH,
        )

    lax.fori_loop(0, 2 * SWEEPS, one_step, 0)

    def give(plane, _):
        for at in range(0, half, term_rows):
            gsend[plane, at : at + term_rows] = terms(0, plane, at, term_rows)
        swap(plane).start()
        return 0

    lax.fori_loop(0, planes, give, 0)

    lax.fori_loop(2 * SWEEPS, 4 * SWEEPS, one_step, 0)

    def finish(plane, _):
        swap(plane).wait_recv()
        for at in range(0, half, term_rows):
            out[plane, at : at + term_rows] = (
                terms(1, plane, at, term_rows) + grecv[plane, at : at + term_rows]
            )
        swap(plane).wait_send()
        return 0

    lax.fori_loop(0, planes, finish, 0)
    for part in range(2):
        for field in range(2):
            wait_sent(part, field, SWEEPS - 1)


def solve_both(fwd, adj, absorb, fsrc, asrc):
    planes, ny, depth = absorb.shape
    half = ny // 2
    span = half + EDGE
    count = lax.axis_size("gx")
    f32 = jnp.float32
    return pl.pallas_call(
        functools.partial(solve_kernel, count, planes, ny, depth),
        out_shape=jax.ShapeDtypeStruct((planes, half, depth), f32),
        in_specs=[pl.BlockSpec(memory_space=pl.ANY)] * 5,
        out_specs=pl.BlockSpec(memory_space=pltpu.VMEM),
        scratch_shapes=[
            pltpu.VMEM((2, 2, 2, planes + 2, span + 16, depth), f32),
            pltpu.VMEM((2, planes, span, depth), f32),
            pltpu.VMEM((2, 2, span, LANES), f32),
            pltpu.VMEM((planes, half, depth), f32),
            pltpu.VMEM((planes, half, depth), f32),
            pltpu.SemaphoreType.DMA((2, 5)),
            pltpu.SemaphoreType.DMA((2, 2, SWEEPS, 2)),
            pltpu.SemaphoreType.DMA((2, 2, SWEEPS, 2)),
            pltpu.SemaphoreType.DMA((planes,)),
            pltpu.SemaphoreType.DMA((planes,)),
        ],
        compiler_params=pltpu.CompilerParams(
            collective_id=0, has_side_effects=True, vmem_limit_bytes=48 * 1024 * 1024
        ),
        cost_estimate=pl.CostEstimate(
            flops=24 * SWEEPS * planes * ny * depth,
            bytes_accessed=14 * planes * ny * depth,
            transcendentals=0,
        ),
    )(fwd, adj, absorb, fsrc, asrc)


def surface_field(start, absorb, source):
    deep = SWEEPS + 1
    count = lax.axis_size("gx")
    top = jnp.transpose(start[:, :, :deep], (0, 2, 1))
    scale = 1.0 / (6.0 + jnp.transpose(absorb[:, :, :deep], (0, 2, 1)))
    packed = jnp.concatenate([top, scale, source[:, None, :]], axis=1)
    forward = [(i, i + 1) for i in range(count - 1)]
    backward = [(target, origin) for origin, target in forward]
    low = lax.ppermute(packed[-SWEEPS:], "gx", forward)
    high = lax.ppermute(packed[:SWEEPS], "gx", backward)
    packed = jnp.concatenate([low, packed, high], axis=0)
    field, scale, drive = packed[:, :deep], packed[:, deep : 2 * deep], packed[:, 2 * deep :]
    drive = jnp.pad(drive, ((0, 0), (0, deep - 1), (0, 0)))
    for sweep in range(SWEEPS):
        side = jnp.pad(field, 1)
        beside = side[2:, 1:-1, 1:-1] + side[:-2, 1:-1, 1:-1]
        beside = beside + side[1:-1, 1:-1, 2:] + side[1:-1, 1:-1, :-2]
        beside = beside + side[1:-1, 2:, 1:-1] + side[1:-1, :-2, 1:-1]
        field = field + sweep_weight(sweep) * ((beside + drive) * scale - field)
    return field[SWEEPS:-SWEEPS, 0]


def shards(pattern_index, patterns, freq_bins, absorption, forward_start, adjoint_start, measured):
    high = lax.Precision.HIGHEST
    planes = forward_start.shape[1]
    total_x = lax.axis_size("gx") * planes
    bins = freq_bins.shape[0]
    source = lax.dynamic_index_in_dim(patterns, pattern_index[0], 0, keepdims=False)
    surface = surface_field(forward_start[0], absorption, source)
    columns = lax.all_to_all(surface, "gx", split_axis=1, concat_axis=0, tiled=True)
    cos_table, sin_table = make_tables(freq_bins, jnp.arange(total_x, dtype=jnp.int32), total_x)
    table = jnp.concatenate([cos_table, -sin_table], axis=0)
    model = jnp.dot(table, columns, precision=high)
    misfit = model - measured[0].reshape(2 * bins, -1)
    back = lax.dot_general(misfit, table, (((0,), (0,)), ((), ())), precision=high)
    drive = lax.all_to_all(back, "gx", split_axis=1, concat_axis=0, tiled=True)
    widen = ((0, 0), (0, LANES - planes))
    gradient = solve_both(
        forward_start[0],
        adjoint_start[0],
        absorption,
        jnp.pad(source.T, widen),
        jnp.pad(drive, widen),
    )
    return (gradient, model.reshape(measured.shape))


def solution(mesh):
    placed = (
        P("pat"),
        P(None, "gx", None),
        P(),
        P("gx", None, None),
        P("pat", "gx", None, None),
        P("pat", "gx", None, None),
        P("pat", None, None, "gx"),
    )
    return jax.shard_map(
        shards,
        mesh=mesh,
        in_specs=placed,
        out_specs=(P("gx", "pat", None), P("pat", None, None, "gx")),
        check_vma=False,
    )
```

profile of v0, /device:TPU:9, one launch (start us, length us, event | category | flops | bytes accessed | tf_op | source)
XLA Modules:
  0.0 154.3 jit_solution(14876541798702341757)
XLA Ops:
  0.6 0.0 copy-start
  1.3 4.4 %slice_bitcast_fusion = f32[8,5,1024]{1,2,0:T(8,128)} fusion(f32[8,1024,128]{2,1,0:T(8,128)} %bitcast.48), kind=kLoop, calls=%fused_computation | loop fusion | bytes 327680 | tf_op jit(solution)/shard_map/transpose | solution.py:305
  5.8 2.9 %copy.18 = f32[8,5,1024]{2,0,1:T(8,128)S(1)} copy(f32[8,5,1024]{1,2,0:T(8,128)} %slice_bitcast_fusion) | data formatting | bytes 327680 | tf_op jit(solution)/shard_map/transpose | solution.py:305
  8.6 2.9 %copy.23 = f32[8,1024,5]{1,0,2:T(8,128)S(1)} copy(f32[8,1024,5]{2,1,0:T(8,128)} %bitcast.50) | data formatting | bytes 327680
  11.6 0.0 copy-done
  11.7 0.1 fusion.52
  11.7 0.0 copy-start.2
  11.7 3.7 %collective-permute-start = (f32[4,11,1024]{2,0,1:T(4,128)S(1)}, f32[4,11,1024]{2,0,1:T(4,128)S(1)}, u32[]{:S(2)}, u32[]{:S(2)}) collective-permute-start(f32[4,11,1024]{2,0,1:T(4,128)S(1)} %get-tuple-element.5), channel_id=1, source_target_pairs={{0,1},{1,2},{2,3},{3,4},{4,5},{5,6},{6,7},{7,8},{8,9},{9,10},{10,1... | collective-permute-start | bytes 540680 | tf_op jit(solution)/shard_map/ppermute | solution.py:310
  15.5 0.0 copy-start.1
  15.5 1.9 %collective-permute-start.1 = (f32[4,11,1024]{2,0,1:T(4,128)S(1)}, f32[4,11,1024]{2,0,1:T(4,128)S(1)}, u32[]{:S(2)}, u32[]{:S(2)}) collective-permute-start(f32[4,11,1024]{2,0,1:T(4,128)S(1)} %get-tuple-element.6), channel_id=1, source_target_pairs={{1,0},{2,1},{3,2},{4,3},{5,4},{6,5},{7,6},{8,7},{9,8},{10,9},{11,1... | collective-permute-start | bytes 540680 | tf_op jit(solution)/shard_map/ppermute | solution.py:311
  17.4 0.5 collective-permute-done
  17.9 4.4 %collective-permute-done.1 = f32[4,11,1024]{2,0,1:T(4,128)S(1)} collective-permute-done((f32[4,11,1024]{2,0,1:T(4,128)S(1)}, f32[4,11,1024]{2,0,1:T(4,128)S(1)}, u32[]{:S(2)}, u32[]{:S(2)}) %collective-permute-start.1) | collective-permute-done | bytes 180256 | tf_op jit(solution)/shard_map/ppermute | solution.py:311
  22.3 0.1 pad_maximum_fusion
  22.5 0.3 fusion.9
  22.7 0.2 fusion.19
  23.0 0.2 fusion.29
  23.2 0.2 fusion.33
  23.5 0.1 all_to_all.28
  23.6 0.7 reshape.17
  24.3 5.9 %all-to-all-start = ((f32[16,1,512]{2,1,0:T(1,128)}), f32[16,1,512]{2,1,0:T(1,128)S(1)}, u32[]{:S(2)}, u32[]{:S(2)}) async-start(f32[16,1,512]{2,1,0:T(1,128)} %reshape.17), calls=%async_computation | async-start | bytes 65536 | tf_op jit(solution)/shard_map/all_to_all | solution.py:331
  30.3 0.0 copy-done.2
  30.3 0.1 cosine_multiply_fusion
  30.4 4.9 %all-to-all-done = f32[16,1,512]{2,1,0:T(1,128)S(1)} async-done(((f32[16,1,512]{2,1,0:T(1,128)}), f32[16,1,512]{2,1,0:T(1,128)S(1)}, u32[]{:S(2)}, u32[]{:S(2)}) %all-to-all-start) | async-done | bytes 32800 | tf_op jit(solution)/shard_map/all_to_all | solution.py:331
  35.3 0.6 broadcast.53
  35.9 0.8 reduce
  36.6 0.1 reshape.18
  36.7 0.0 copy-done.1
  36.7 0.8 bitcast_subtract_fusion
  37.5 0.3 fusion.53
  37.8 0.7 reshape.19
  38.5 5.0 %all-to-all-start.1 = ((f32[16,1,512]{2,1,0:T(1,128)}), f32[16,1,512]{2,1,0:T(1,128)S(1)}, u32[]{:S(2)}, u32[]{:S(2)}) async-start(f32[16,1,512]{2,1,0:T(1,128)} %reshape.19), calls=%async_computation.1 | async-start | bytes 65536 | tf_op jit(solution)/shard_map/all_to_all | solution.py:337
  43.5 0.2 copy.16
  43.8 4.8 %all-to-all-done.1 = f32[16,1,512]{2,1,0:T(1,128)S(1)} async-done(((f32[16,1,512]{2,1,0:T(1,128)}), f32[16,1,512]{2,1,0:T(1,128)S(1)}, u32[]{:S(2)}, u32[]{:S(2)}) %all-to-all-start.1) | async-done | bytes 32800 | tf_op jit(solution)/shard_map/all_to_all | solution.py:337
  48.6 0.8 reduce.1
  49.4 0.1 reshape.20
  49.5 0.2 copy.21
  49.7 103.3 %shard_map.86 = f32[8,512,128]{2,1,0:T(8,128)S(1)} custom-call(f32[8,1024,128]{2,1,0:T(8,128)} %bitcast.49, f32[8,1024,128]{2,1,0:T(8,128)} %bitcast.51, f32[8,1024,128]{2,1,0:T(8,128)} %absorb.1, f32[1024,128]{1,0:T(8,128)S(1)} %pad.24.fsrc, f32[1024,128]{1,0:T(8,128)S(1)} %pad.30.asrc), custom_call_target="tpu_custom_call" | custom-call | flops 100663296 | bytes 14680064 | tf_op jit(solution)/shard_map/pallas_call | solution.py:274
  153.0 1.3 copy.28
  (10 shorter events, 0.2 us)
Async XLA Ops:
  0.6 11.0 %copy-start = (f32[8,8,1024]{2,1,0:T(8,128)S(1)}, f32[8,8,1024]{2,1,0:T(8,128)}, u32[]{:S(2)}) copy-start(f32[8,8,1024]{2,1,0:T(8,128)} %param.8) | copy-start | bytes 786436
  11.7 18.5 %copy-start.2 = (s32[16]{0:T(128)S(1)}, s32[16]{0:T(128)}, u32[]{:S(2)}) copy-start(s32[16]{0:T(128)} %param.9) | copy-start | bytes 196
  11.7 6.1 %collective-permute-start = (f32[4,11,1024]{2,0,1:T(4,128)S(1)}, f32[4,11,1024]{2,0,1:T(4,128)S(1)}, u32[]{:S(2)}, u32[]{:S(2)}) collective-permute-start(f32[4,11,1024]{2,0,1:T(4,128)S(1)} %get-tuple-element.5), channel_id=1, source_target_pairs={{0,1},{1,2},{2,3},{3,4},{4,5},{5,6},{6,7},{7,8},{8,9},{9,10},{10,1... | collective-permute-start | bytes 540680 | tf_op jit(solution)/shard_map/ppermute | solution.py:310
  15.5 21.3 %copy-start.1 = (f32[1,2,16,64]{3,2,1,0:T(8,128)S(1)}, f32[1,2,16,64]{3,2,1,0:T(8,128)}, u32[]{:S(2)}) copy-start(f32[1,2,16,64]{3,2,1,0:T(8,128)} %param.13) | copy-start | bytes 24580
  15.5 6.8 %collective-permute-start.1 = (f32[4,11,1024]{2,0,1:T(4,128)S(1)}, f32[4,11,1024]{2,0,1:T(4,128)S(1)}, u32[]{:S(2)}, u32[]{:S(2)}) collective-permute-start(f32[4,11,1024]{2,0,1:T(4,128)S(1)} %get-tuple-element.6), channel_id=1, source_target_pairs={{1,0},{2,1},{3,2},{4,3},{5,4},{6,5},{7,6},{8,7},{9,8},{10,9},{11,1... | collective-permute-start | bytes 540680 | tf_op jit(solution)/shard_map/ppermute | solution.py:311
  24.3 11.0 %all-to-all-start = ((f32[16,1,512]{2,1,0:T(1,128)}), f32[16,1,512]{2,1,0:T(1,128)S(1)}, u32[]{:S(2)}, u32[]{:S(2)}) async-start(f32[16,1,512]{2,1,0:T(1,128)} %reshape.17), calls=%async_computation | async-start | bytes 65536 | tf_op jit(solution)/shard_map/all_to_all | solution.py:331
  38.5 10.1 %all-to-all-start.1 = ((f32[16,1,512]{2,1,0:T(1,128)}), f32[16,1,512]{2,1,0:T(1,128)S(1)}, u32[]{:S(2)}, u32[]{:S(2)}) async-start(f32[16,1,512]{2,1,0:T(1,128)} %reshape.19), calls=%async_computation.1 | async-start | bytes 65536 | tf_op jit(solution)/shard_map/all_to_all | solution.py:337
where the time goes:
time: 155 us; the launch traced here: 154 us
  Pallas kernels  103 us (66%)
  starting transfers between devices  16.6 us (11%)
  waiting for transfers between devices  14.6 us (9%)
  local copies, waits for them, and re-layouts  14.4 us (9%)
  other arithmetic  2.86 us (2%)
  between operations  1.55 us (1%)
    pallas_call x1, Pallas kernels, solve_both(): pl.pallas_call(functools.partial(solve_kernel, count, planes, ny, depth),...  103 us
    transpose x2, local copies, waits for them, and re-layouts, surface_field(): top = jnp.transpose(start[:, :, :deep], (0, 2, 1))  7.31 us
    all_to_all x1, starting transfers between devices, shards(): lax.all_to_all(surface, 'gx', split_axis=1, concat_axis=0, tiled=True)  5.94 us
    unnamed x12, local copies, waits for them, and re-layouts  5.82 us
    all_to_all x1, starting transfers between devices, shards(): drive = lax.all_to_all(back, 'gx', split_axis=1, concat_axis=0, tiled=True)  5.02 us
    all_to_all x1, waiting for transfers between devices, shards(): lax.all_to_all(surface, 'gx', split_axis=1, concat_axis=0, tiled=True)  4.88 us
    all_to_all x1, waiting for transfers between devices, shards(): drive = lax.all_to_all(back, 'gx', split_axis=1, concat_axis=0, tiled=True)  4.82 us
    ppermute x1, waiting for transfers between devices, surface_field(): high = lax.ppermute(packed[:SWEEPS], 'gx', backward)  4.41 us
  transfers between devices with their start and end apart: 4, of which 4 were waited for; matrix products, arithmetic and copies ran while one was open for 0% of the time, Pallas kernels for 0%

commit v1 on v0

v1 whole, which is shorter than its diff:
```python
import functools
import math

import jax
import jax.numpy as jnp
from jax import lax
from jax.experimental import pallas as pl
from jax.experimental.pallas import tpu as pltpu
from jax.sharding import PartitionSpec as P

SWEEPS = 4
EDGE = 8
LANES = 128
MESH = pl.DeviceIdType.MESH


def sweep_weight(sweep):
    return 1.0 / (1.25 + 0.75 * math.cos(math.pi * (2 * sweep + 1) / (2 * SWEEPS)))


def make_tables(freq_bins, positions, total_x):
    phase = freq_bins[:, None] * positions[None, :] % total_x
    angle = 2.0 * math.pi / total_x * phase.astype(jnp.float32)
    return (jnp.cos(angle) / math.sqrt(total_x), jnp.sin(angle) / math.sqrt(total_x))


def chunk_rows(rows):
    tiles = rows // 8
    for size in range(min(tiles, 13), 0, -1):
        if tiles % size == 0:
            return size * 8
    return 8


def solve_kernel(
    count, planes, ny, depth,
    fwd, adj, absorb, fsrc, pattern, measured, table, own_table, out, model,
    buf, inv, srcs, given, layer, other_layer, surfaces, images, modelled, drive,
    load_sems, send_sems, recv_sems, give_send, give_recv, layer_send, layer_recv,
    all_send, all_recv, pat_send, pat_recv,
):
    half = ny // 2
    span = half + EDGE
    width = ny // count
    me = lax.axis_index("gx")
    pat = lax.axis_index("pat")
    last = count - 1

    first_row = (
        pl.multiple_of((1 - pat) * (half - EDGE), 8),
        pl.multiple_of(pat * (half - EDGE), 8),
    )
    skip = (pl.multiple_of((1 - pat) * EDGE, 8), pl.multiple_of(pat * EDGE, 8))
    half_at = (pl.multiple_of((1 - pat) * half, LANES), pl.multiple_of(pat * half, LANES))
    inner = (pl.ds(1, planes), pl.ds(8, span))

    loads = []
    for part in range(2):
        rows = pl.ds(first_row[part], span)
        group = (
            pltpu.make_async_copy(
                fwd.at[:, rows], buf.at[(part, 0, 0) + inner], load_sems.at[part, 0]
            ),
            pltpu.make_async_copy(absorb.at[:, rows], inv.at[part], load_sems.at[part, 1]),
            pltpu.make_async_copy(fsrc.at[rows], srcs.at[part, 0], load_sems.at[part, 2]),
        )
        for copy in group:
            copy.start()
        loads.append(group)
    adj_load = pltpu.make_async_copy(
        adj.at[:, pl.ds(first_row[1], span)], buf.at[(1, 1, 0) + inner], load_sems.at[1, 3]
    )
    adj_load.start()

    barrier = pltpu.get_barrier_semaphore()
    pl.semaphore_signal(barrier, inc=1, device_id={"pat": 1 - pat}, device_id_type=MESH)

    def greet(step, _):
        other = lax.rem(me + step, count)
        pl.semaphore_signal(barrier, inc=1, device_id={"gx": other}, device_id_type=MESH)
        return 0

    lax.fori_loop(1, count, greet, 0)

    edge_rows = jnp.zeros((8, depth), jnp.float32)

    def clear_edges(i, _):
        part, field, slot, plane = i // (4 * planes), i // (2 * planes) % 2, i // planes % 2, i % planes
        buf[part, field, slot, plane + 1, 0:8] = edge_rows
        buf[part, field, slot, plane + 1, 8 + span : 16 + span] = edge_rows
        return 0

    lax.fori_loop(0, 8 * planes, clear_edges, 0)

    def clear_plane(plane, layer_at):
        def body(i, _):
            buf[i // 4, i // 2 % 2, i % 2, plane] = jnp.zeros((16 + span, depth), jnp.float32)
            return 0

        lax.fori_loop(0, 8, body, 0)

        def layers(i, _):
            layer[i % 2, layer_at + i // 2] = jnp.zeros((8, ny), jnp.float32)
            return 0

        lax.fori_loop(0, 2 * SWEEPS, layers, 0)

    @pl.when(me == 0)
    def _():
        clear_plane(0, 0)

    @pl.when(me == last)
    def _():
        clear_plane(planes + 1, SWEEPS + planes)

    images[me] = measured[...]
    pl.semaphore_wait(barrier, count)

    rows_held = pl.ds(8, span)

    def face(part, field, sweep, side):
        slot = sweep % 2
        return pltpu.make_async_remote_copy(
            src_ref=buf.at[part, field, slot, 1 if side == 0 else planes, rows_held],
            dst_ref=buf.at[part, field, slot, planes + 1 if side == 0 else 0, rows_held],
            send_sem=send_sems.at[part, field, sweep, side],
            recv_sem=recv_sems.at[part, field, sweep, side],
            device_id={"gx": me - 1 if side == 0 else me + 1},
            device_id_type=MESH,
        )

    def layers_to(which, side):
        return pltpu.make_async_remote_copy(
            src_ref=layer.at[which, pl.ds(SWEEPS if side == 0 else planes, SWEEPS)],
            dst_ref=layer.at[which, pl.ds(SWEEPS + planes if side == 0 else 0, SWEEPS)],
            send_sem=layer_send.at[which, side],
            recv_sem=layer_recv.at[which, side],
            device_id={"gx": me - 1 if side == 0 else me + 1},
            device_id_type=MESH,
        )

    def by_side(low, high):
        @pl.when(me > 0)
        def _():
            low()

        @pl.when(me < last)
        def _():
            high()

    def send_faces(part, field, sweep):
        by_side(
            lambda: face(part, field, sweep, 0).start(), lambda: face(part, field, sweep, 1).start()
        )

    def wait_sent(part, field, sweep):
        by_side(
            lambda: face(part, field, sweep, 0).wait_send(),
            lambda: face(part, field, sweep, 1).wait_send(),
        )

    def wait_faces(part, field, sweep):
        by_side(
            lambda: face(part, field, sweep, 1).wait_recv(),
            lambda: face(part, field, sweep, 0).wait_recv(),
        )

    def to_all(kind, block, step, sender):
        return pltpu.make_async_remote_copy(
            src_ref=block.at[sender],
            dst_ref=block.at[sender],
            send_sem=all_send.at[kind, step],
            recv_sem=all_recv.at[kind, sender],
            device_id={"gx": lax.rem(me + step, count)},
            device_id_type=MESH,
        )

    def spread(kind, block):
        def body(step, _):
            to_all(kind, block, step, me).start()
            return 0

        lax.fori_loop(1, count, body, 0)

    def collect(kind, block):
        def body(step, _):
            to_all(kind, block, step, lax.rem(me + count - step, count)).wait_recv()
            to_all(kind, block, step, me).wait_send()
            return 0

        lax.fori_loop(1, count, body, 0)

    def to_pattern(src, dst, sem):
        return pltpu.make_async_remote_copy(
            src_ref=src,
            dst_ref=dst,
            send_sem=pat_send.at[sem],
            recv_sem=pat_recv.at[sem],
            device_id={"pat": 1 - pat},
            device_id_type=MESH,
        )

    start_swap = to_pattern(
        adj.at[:, pl.ds(first_row[0], span)], buf.at[(0, 1, 0) + inner], 0
    )
    drive_swap = to_pattern(drive.at[pl.ds(first_row[0], span)], srcs.at[0, 1], 1)

    def give(plane):
        return pltpu.make_async_remote_copy(
            src_ref=buf.at[0, 0, SWEEPS % 2, plane + 1, pl.ds(8 + skip[0], half)],
            dst_ref=given.at[plane],
            send_sem=give_send.at[plane],
            recv_sem=give_recv.at[plane],
            device_id={"pat": 1 - pat},
            device_id_type=MESH,
        )

    step_rows = chunk_rows(span)

    def invert(part):
        def body(plane, _):
            for at in range(0, span, step_rows):
                inv[part, plane, at : at + step_rows] = 1.0 / (
                    6.0 + inv[part, plane, at : at + step_rows]
                )
            return 0

        lax.fori_loop(0, planes, body, 0)

    for part in range(2):
        loads[part][0].wait()
        if part == 0:
            send_faces(0, 0, 0)
            start_swap.start()
        for copy in loads[part][1:]:
            copy.wait()
        invert(part)

    pick = (
        lax.broadcasted_iota(jnp.int32, (8, depth), 0)
        == lax.broadcasted_iota(jnp.int32, (8, depth), 1)
    ).astype(jnp.float32)
    high = lax.Precision.HIGHEST
    over_lanes = (((1,), (1,)), ((), ()))

    def lift(plane, _):
        for part in range(2):
            lanes = pl.ds(half_at[part], half)
            block = buf[part, 0, 0, plane + 1, pl.ds(8 + skip[part], half)]
            layer[0, SWEEPS + plane, :, lanes] = lax.dot_general(
                pick, block, over_lanes, precision=high, preferred_element_type=jnp.float32
            )
            block = inv[part, plane, pl.ds(skip[part], half)]
            layer[1, SWEEPS + plane, :, lanes] = lax.dot_general(
                pick, block, over_lanes, precision=high, preferred_element_type=jnp.float32
            )
        layer[1, SWEEPS + plane, 7:8] = pattern[pl.ds(plane, 1)]
        return 0

    lax.fori_loop(0, planes, lift, 0)
    for which in range(2):
        by_side(lambda: layers_to(which, 0).start(), lambda: layers_to(which, 1).start())
    send_faces(1, 0, 0)
    spread(0, images)
    adj_load.wait()

    lane = lax.broadcasted_iota(jnp.int32, (step_rows, depth), 1)
    top = lane == 0
    bottom = lane == depth - 1

    def update(part, field, sweep, plane, weight):
        now, later = sweep % 2, (sweep + 1) % 2
        scales = jnp.maximum(part, field)
        for at in range(0, span, step_rows):
            here = pl.ds(8 + at, step_rows)
            center = buf[part, field, now, plane, here]
            column = srcs[part, field, pl.ds(at, step_rows)]
            column = pltpu.roll(column, lax.rem(depth + 1 - plane, depth), 1)
            beside = buf[part, field, now, plane - 1, here] + buf[part, field, now, plane + 1, here]
            beside = beside + buf[part, field, now, plane, pl.ds(7 + at, step_rows)]
            beside = beside + buf[part, field, now, plane, pl.ds(9 + at, step_rows)]
            beside = beside + jnp.where(top, column, pltpu.roll(center, 1, 1))
            beside = beside + jnp.where(bottom, 0.0, pltpu.roll(center, depth - 1, 1))
            scale = inv[scales, plane - 1, pl.ds(at, step_rows)]
            buf[part, field, later, plane, here] = center + weight * (beside * scale - center)

    def one_step(index, _):
        part = index % 2
        stage = index // 2
        field, sweep = stage // SWEEPS, stage % SWEEPS
        weight = jnp.float32(sweep_weight(0))
        for other in range(1, SWEEPS):
            weight = jnp.where(sweep == other, jnp.float32(sweep_weight(other)), weight)
        wait_faces(part, field, sweep)

        @pl.when(sweep > 0)
        def _():
            wait_sent(part, field, sweep - 1)

        def outer(i, _):
            update(part, field, sweep, 1 + i * (planes - 1), weight)
            return 0

        lax.fori_loop(0, 2, outer, 0)
        coming = stage + 1

        @pl.when(index == 2 * (SWEEPS - 1))
        def _():
            start_swap.wait_recv()

        @pl.when(coming < 2 * SWEEPS)
        def _():
            send_faces(part, coming // SWEEPS, coming % SWEEPS)

        def within(plane, _):
            update(part, field, sweep, plane, weight)
            return 0

        lax.fori_loop(2, planes, within, 0)
        return 0

    lax.fori_loop(0, 2, one_step, 0)

    for which in range(2):
        by_side(lambda: layers_to(which, 1).wait_recv(), lambda: layers_to(which, 0).wait_recv())
        by_side(lambda: layers_to(which, 0).wait_send(), lambda: layers_to(which, 1).wait_send())
    row_of = lax.broadcasted_iota(jnp.int32, (8, ny), 0)
    place = lax.broadcasted_iota(jnp.int32, (8, ny), 1)

    def shallow(source, target, weight):
        def body(plane, _):
            center = source[plane]
            scale = layer[1, plane]
            beside = source[plane - 1] + source[plane + 1]
            beside = beside + jnp.where(place == 0, 0.0, pltpu.roll(center, 1, 1))
            beside = beside + jnp.where(place == ny - 1, 0.0, pltpu.roll(center, ny - 1, 1))
            beside = beside + jnp.where(row_of == 0, pltpu.roll(scale, 1, 0), pltpu.roll(center, 1, 0))
            beside = beside + pltpu.roll(center, 7, 0)
            target[plane] = center + weight * (beside * scale - center)
            return 0

        return body

    for sweep in range(SWEEPS):
        ends = (layer.at[0], other_layer)
        lax.fori_loop(
            1 + sweep,
            planes + 2 * SWEEPS - 1 - sweep,
            shallow(ends[sweep % 2], ends[(sweep + 1) % 2], sweep_weight(sweep)),
            0,
        )
    for plane in range(planes):
        surfaces[me, plane : plane + 1] = layer[0, SWEEPS + plane, 0:1]
    spread(1, surfaces)

    lax.fori_loop(2, 4, one_step, 0)

    collect(0, images)
    collect(1, surfaces)
    block_rows = max(LANES, width)
    senders = block_rows // width

    def transform(i, _):
        at = pl.multiple_of(i * block_rows, block_rows)
        strip = surfaces[:, :, pl.ds(at, block_rows)].reshape(count * planes, block_rows)
        image = jnp.dot(
            strip.T, table[...], precision=high, preferred_element_type=jnp.float32
        )
        modelled[pl.ds(at, block_rows)] = image
        misfit = image - images[pl.ds(i * senders, senders)].reshape(block_rows, LANES)
        drive[pl.ds(at, block_rows)] = jnp.dot(
            misfit, own_table[...], precision=high, preferred_element_type=jnp.float32
        )
        return 0

    lax.fori_loop(0, ny // block_rows, transform, 0)
    drive_swap.start()
    model[...] = modelled[pl.ds(pl.multiple_of(me * width, width), width)]
    srcs[1, 1] = drive[pl.ds(first_row[1], span)]

    lax.fori_loop(4, 2 * SWEEPS, one_step, 0)
    for plane in range(planes):
        give(plane).start()
    drive_swap.wait_recv()
    lax.fori_loop(2 * SWEEPS, 4 * SWEEPS, one_step, 0)

    term_rows = chunk_rows(half)
    slot = SWEEPS % 2

    def finish(plane, _):
        give(plane).wait_recv()
        for at in range(0, half, term_rows):
            where = pl.ds(8 + skip[1] + at, term_rows)
            ours = buf[1, 0, slot, plane + 1, where] * buf[1, 1, slot, plane + 1, where]
            theirs = given[plane, pl.ds(at, term_rows)] * buf[0, 1, slot, plane + 1, where]
            out[plane, at : at + term_rows] = -(ours + theirs)
        give(plane).wait_send()
        return 0

    lax.fori_loop(0, planes, finish, 0)
    start_swap.wait_send()
    drive_swap.wait_send()
    for part in range(2):
        for field in range(2):
            wait_sent(part, field, SWEEPS - 1)


def solve_both(fwd, adj, absorb, fsrc, pattern, measured, table, own_table):
    planes, ny, depth = absorb.shape
    half = ny // 2
    span = half + EDGE
    count = lax.axis_size("gx")
    f32 = jnp.float32
    dma = pltpu.SemaphoreType.DMA
    return pl.pallas_call(
        functools.partial(solve_kernel, count, planes, ny, depth),
        out_shape=(
            jax.ShapeDtypeStruct((planes, half, depth), f32),
            jax.ShapeDtypeStruct((ny // count, LANES), f32),
        ),
        in_specs=[pl.BlockSpec(memory_space=pl.ANY)] * 4
        + [pl.BlockSpec(memory_space=pltpu.VMEM)] * 4,
        out_specs=[pl.BlockSpec(memory_space=pltpu.VMEM)] * 2,
        scratch_shapes=[
            pltpu.VMEM((2, 2, 2, planes + 2, span + 16, depth), f32),
            pltpu.VMEM((2, planes, span, depth), f32),
            pltpu.VMEM((2, 2, span, LANES), f32),
            pltpu.VMEM((planes, half, depth), f32),
            pltpu.VMEM((2, planes + 2 * SWEEPS, 8, ny), f32),
            pltpu.VMEM((planes + 2 * SWEEPS, 8, ny), f32),
            pltpu.VMEM((count, planes, ny), f32),
            pltpu.VMEM((count, ny // count, LANES), f32),
            pltpu.VMEM((ny, LANES), f32),
            pltpu.VMEM((ny, LANES), f32),
            dma((2, 4)),
            dma((2, 2, SWEEPS, 2)),
            dma((2, 2, SWEEPS, 2)),
            dma((planes,)),
            dma((planes,)),
            dma((2, 2)),
            dma((2, 2)),
            dma((2, count)),
            dma((2, count)),
            dma((2,)),
            dma((2,)),
        ],
        compiler_params=pltpu.CompilerParams(
            collective_id=0, has_side_effects=True, vmem_limit_bytes=48 * 1024 * 1024
        ),
        cost_estimate=pl.CostEstimate(
            flops=24 * SWEEPS * planes * ny * depth,
            bytes_accessed=14 * planes * ny * depth,
            transcendentals=0,
        ),
    )(fwd, adj, absorb, fsrc, pattern, measured, table, own_table)


def shards(pattern_index, patterns, freq_bins, absorption, forward_start, adjoint_start, measured):
    planes = forward_start.shape[1]
    total_x = lax.axis_size("gx") * planes
    bins = freq_bins.shape[0]
    source = lax.dynamic_index_in_dim(patterns, pattern_index[0], 0, keepdims=False)
    positions = jnp.arange(total_x, dtype=jnp.int32)
    cos_table, sin_table = make_tables(freq_bins, positions, total_x)
    table = jnp.concatenate([cos_table, -sin_table], axis=0)
    table = jnp.pad(table, ((0, LANES - 2 * bins), (0, 0)))
    own_table = lax.dynamic_slice_in_dim(table, lax.axis_index("gx") * planes, planes, axis=1)
    widen = ((0, 0), (0, LANES - planes))
    gradient, model = solve_both(
        forward_start[0],
        adjoint_start[0],
        absorption,
        jnp.pad(source.T, widen),
        source,
        jnp.pad(measured[0].reshape(2 * bins, -1).T, ((0, 0), (0, LANES - 2 * bins))),
        table.T,
        jnp.pad(own_table, widen),
    )
    return (gradient, model[:, : 2 * bins].T.reshape(measured.shape))


def solution(mesh):
    placed = (
        P("pat"),
        P(None, "gx", None),
        P(),
        P("gx", None, None),
        P("pat", "gx", None, None),
        P("pat", "gx", None, None),
        P("pat", None, None, "gx"),
    )
    return jax.shard_map(
        shards,
        mesh=mesh,
        in_specs=placed,
        out_specs=(P("gx", "pat", None), P("pat", None, None, "gx")),
        check_vma=False,
    )
```

time: 155 us -> 137 us (0.88)
  Pallas kernels: 103 us -> 130 us
  starting transfers between devices: 16.6 us -> 0 us
  waiting for transfers between devices: 14.6 us -> 0 us
  local copies, waits for them, and re-layouts: 14.4 us -> 4 us
  other arithmetic: 2.86 us -> 0.79 us
    pallas_call x1, Pallas kernels: 103 us -> 130 us  [solve_both(): pl.pallas_call(functools.partial(solve_kernel, count, planes, ny, depth),...]
    all_to_all x2 -> x0, starting transfers between devices: 11 us -> none  [the longest x1 5.94 us: shards(): lax.all_to_all(surface, 'gx', split_axis=1, concat_axis=0, tiled=True)]
    all_to_all x2 -> x0, waiting for transfers between devices: 9.7 us -> none  [the longest x1 4.88 us: shards(): lax.all_to_all(surface, 'gx', split_axis=1, concat_axis=0, tiled=True)]
    transpose x2 -> x3, local copies, waits for them, and re-layouts: 7.31 us -> 0.77 us  [the longest x2 0.68 us: shards(): return (gradient, model[:, :2 * bins].T.reshape(measured.shape))]
    ppermute x2 -> x0, starting transfers between devices: 5.63 us -> none  [the longest x1 3.71 us: surface_field(): low = lax.ppermute(packed[-SWEEPS:], 'gx', forward)]
    ppermute x2 -> x0, waiting for transfers between devices: 4.88 us -> none  [the longest x1 4.41 us: surface_field(): high = lax.ppermute(packed[:SWEEPS], 'gx', backward)]
    unnamed x12 -> x2, local copies, waits for them, and re-layouts: 5.82 us -> 1.52 us
  transfers between devices with their start and end apart: 4 -> 0, of which waited for: 4 -> 0; matrix products, arithmetic and copies ran while one was open for 0% -> 0% of each run, Pallas kernels for 0% -> 0%
where the time goes in v1:
time: 137 us; the launch traced here: 136 us
  Pallas kernels  130 us (95%)
  local copies, waits for them, and re-layouts  4 us (3%)
    pallas_call x1, Pallas kernels, solve_both(): pl.pallas_call(functools.partial(solve_kernel, count, planes, ny, depth),...  130 us

profile of v1, /device:TPU:9, one launch (start us, length us, event | category | flops | bytes accessed | tf_op | source)
XLA Modules:
  0.0 136.4 jit_solution(13491353282725379435)
XLA Ops:
  1.3 0.8 cosine_multiply_fusion
  2.1 0.8 copy.13
  2.9 0.8 dynamic-slice_bitcast_fusion.1
  3.7 0.1 constant_dynamic-slice_fusion
  3.8 0.1 copy.15.table
  3.9 0.2 copy.17
  4.1 130.3 %shard_map.86 = (f32[8,512,128]{2,1,0:T(8,128)S(1)}, f32[64,128]{1,0:T(8,128)S(1)}) custom-call(f32[8,1024,128]{2,1,0:T(8,128)} %bitcast.18, f32[8,1024,128]{2,1,0:T(8,128)} %bitcast.19, f32[8,1024,128]{2,1,0:T(8,128)} %absorb.1, f32[1024,128]{1,0:T(8,128)S(1)} %pad.16.clone.fsrc, f32[8,1024]{1,0:T(8,128)S(1)} %get-tuple-element.8.pattern, ...), custom_call_target="tpu_custom_call" | custom-call | flops 100663296 | bytes 14680064 | tf_op jit(solution)/shard_map/pallas_call | solution.py:415
  134.4 0.7 copy.16
  135.1 1.3 copy.20
  (5 shorter events, 0.1 us)

commit v2 on v1

--- a/solution.py
+++ b/solution.py
@@ -22,14 +22,6 @@
     phase = freq_bins[:, None] * positions[None, :] % total_x
     angle = 2.0 * math.pi / total_x * phase.astype(jnp.float32)
     return (jnp.cos(angle) / math.sqrt(total_x), jnp.sin(angle) / math.sqrt(total_x))
-
-
-def chunk_rows(rows):
-    tiles = rows // 8
-    for size in range(min(tiles, 13), 0, -1):
-        if tiles % size == 0:
-            return size * 8
-    return 8
 
 
 def solve_kernel(
@@ -215,7 +207,7 @@
             device_id_type=MESH,
         )
 
-    step_rows = chunk_rows(span)
+    step_rows = span
 
     def invert(part):
         def body(plane, _):
@@ -236,31 +228,37 @@
             copy.wait()
         invert(part)
 
-    pick = (
-        lax.broadcasted_iota(jnp.int32, (8, depth), 0)
-        == lax.broadcasted_iota(jnp.int32, (8, depth), 1)
-    ).astype(jnp.float32)
     high = lax.Precision.HIGHEST
-    over_lanes = (((1,), (1,)), ((), ()))
-
-    def lift(plane, _):
+    group = LANES // 8
+    eighth = lax.broadcasted_iota(jnp.int32, (LANES, depth), 1) // 8
+
+    def lift(i, _):
         for part in range(2):
-            lanes = pl.ds(half_at[part], half)
-            block = buf[part, 0, 0, plane + 1, pl.ds(8 + skip[part], half)]
-            layer[0, SWEEPS + plane, :, lanes] = lax.dot_general(
-                pick, block, over_lanes, precision=high, preferred_element_type=jnp.float32
-            )
-            block = inv[part, plane, pl.ds(skip[part], half)]
-            layer[1, SWEEPS + plane, :, lanes] = lax.dot_general(
-                pick, block, over_lanes, precision=high, preferred_element_type=jnp.float32
-            )
-        layer[1, SWEEPS + plane, 7:8] = pattern[pl.ds(plane, 1)]
+            at = pl.multiple_of(i * LANES, LANES)
+            pieces = [(0, plane) for plane in range(planes)] + [(1, plane) for plane in range(planes)]
+            for begin in range(0, len(pieces), group):
+                packed = jnp.zeros((LANES, depth), jnp.float32)
+                for spot, (which, plane) in enumerate(pieces[begin : begin + group]):
+                    if which == 0:
+                        block = buf[part, 0, 0, plane + 1, pl.ds(8 + skip[part] + at, LANES)]
+                    else:
+                        block = inv[part, plane, pl.ds(skip[part] + at, LANES)]
+                    if spot > 0:
+                        block = pltpu.roll(block, 8 * spot, 1)
+                    packed = jnp.where(eighth == spot, block, packed)
+                turned = packed.T
+                for spot, (which, plane) in enumerate(pieces[begin : begin + group]):
+                    layer[which, SWEEPS + plane, :, pl.ds(half_at[part] + at, LANES)] = turned[
+                        8 * spot : 8 * spot + 8
+                    ]
         return 0
 
-    lax.fori_loop(0, planes, lift, 0)
+    send_faces(1, 0, 0)
+    lax.fori_loop(0, half // LANES, lift, 0)
+    for plane in range(planes):
+        layer[1, SWEEPS + plane, 7:8] = pattern[plane : plane + 1]
     for which in range(2):
         by_side(lambda: layers_to(which, 0).start(), lambda: layers_to(which, 1).start())
-    send_faces(1, 0, 0)
     spread(0, images)
     adj_load.wait()
 
@@ -327,33 +325,41 @@
     row_of = lax.broadcasted_iota(jnp.int32, (8, ny), 0)
     place = lax.broadcasted_iota(jnp.int32, (8, ny), 1)
 
-    def shallow(source, target, weight):
-        def body(plane, _):
-            center = source[plane]
-            scale = layer[1, plane]
-            beside = source[plane - 1] + source[plane + 1]
-            beside = beside + jnp.where(place == 0, 0.0, pltpu.roll(center, 1, 1))
-            beside = beside + jnp.where(place == ny - 1, 0.0, pltpu.roll(center, ny - 1, 1))
-            beside = beside + jnp.where(row_of == 0, pltpu.roll(scale, 1, 0), pltpu.roll(center, 1, 0))
-            beside = beside + pltpu.roll(center, 7, 0)
-            target[plane] = center + weight * (beside * scale - center)
-            return 0
-
-        return body
-
-    for sweep in range(SWEEPS):
+    def shallow(sweep):
         ends = (layer.at[0], other_layer)
-        lax.fori_loop(
-            1 + sweep,
-            planes + 2 * SWEEPS - 1 - sweep,
-            shallow(ends[sweep % 2], ends[(sweep + 1) % 2], sweep_weight(sweep)),
-            0,
-        )
+        source, target = ends[sweep % 2], ends[(sweep + 1) % 2]
+        first, stop = 1 + sweep, planes + 2 * SWEEPS - 1 - sweep
+        pair = 2 if (stop - first) % 2 == 0 else 1
+
+        def body(i, _):
+            fresh = []
+            for plane in [first + i * pair + more for more in range(pair)]:
+                center = source[plane]
+                scale = layer[1, plane]
+                beside = source[plane - 1] + source[plane + 1]
+                beside = beside + jnp.where(place == 0, 0.0, pltpu.roll(center, 1, 1))
+                beside = beside + jnp.where(place == ny - 1, 0.0, pltpu.roll(center, ny - 1, 1))
+                beside = beside + jnp.where(
+                    row_of == 0, pltpu.roll(scale, 1, 0), pltpu.roll(center, 1, 0)
+                )
+                beside = beside + pltpu.roll(center, 7, 0)
+                fresh.append((plane, center + sweep_weight(sweep) * (beside * scale - center)))
+            for plane, value in fresh:
+                target[plane] = value
+            return 0
+
+        lax.fori_loop(0, (stop - first) // pair, body, 0)
+
+    for sweep in range(SWEEPS // 2):
+        shallow(sweep)
+    lax.fori_loop(2, 3, one_step, 0)
+    for sweep in range(SWEEPS // 2, SWEEPS):
+        shallow(sweep)
     for plane in range(planes):
         surfaces[me, plane : plane + 1] = layer[0, SWEEPS + plane, 0:1]
     spread(1, surfaces)
 
-    lax.fori_loop(2, 4, one_step, 0)
+    lax.fori_loop(3, 6, one_step, 0)
 
     collect(0, images)
     collect(1, surfaces)
@@ -378,13 +384,13 @@
     model[...] = modelled[pl.ds(pl.multiple_of(me * width, width), width)]
     srcs[1, 1] = drive[pl.ds(first_row[1], span)]
 
-    lax.fori_loop(4, 2 * SWEEPS, one_step, 0)
+    lax.fori_loop(6, 2 * SWEEPS, one_step, 0)
     for plane in range(planes):
         give(plane).start()
     drive_swap.wait_recv()
     lax.fori_loop(2 * SWEEPS, 4 * SWEEPS, one_step, 0)
 
-    term_rows = chunk_rows(half)
+    term_rows = half
     slot = SWEEPS % 2
 
     def finish(plane, _):

time: 137 us -> 127 us (0.927)
  Pallas kernels: 130 us -> 120 us
    pallas_call x1, Pallas kernels: 130 us -> 120 us  [solve_both(): pl.pallas_call(functools.partial(solve_kernel, count, planes, ny, depth),...]
where the time goes in v2:
time: 127 us; the launch traced here: 126 us
  Pallas kernels  120 us (94%)
  local copies, waits for them, and re-layouts  4 us (3%)
  between operations  1.34 us (1%)
    pallas_call x1, Pallas kernels, solve_both(): pl.pallas_call(functools.partial(solve_kernel, count, planes, ny, depth),...  120 us

profile of v2, /device:TPU:9, one launch (start us, length us, event | category | flops | bytes accessed | tf_op | source)
XLA Modules:
  0.0 126.3 jit_solution(16218074247312905761)
XLA Ops:
  1.3 0.8 cosine_multiply_fusion
  2.1 0.8 copy.13
  2.9 0.8 dynamic-slice_bitcast_fusion.1
  3.7 0.1 constant_dynamic-slice_fusion
  3.8 0.1 copy.15.table
  3.9 0.2 copy.17
  4.1 120.2 %shard_map.86 = (f32[8,512,128]{2,1,0:T(8,128)S(1)}, f32[64,128]{1,0:T(8,128)S(1)}) custom-call(f32[8,1024,128]{2,1,0:T(8,128)} %bitcast.18, f32[8,1024,128]{2,1,0:T(8,128)} %bitcast.19, f32[8,1024,128]{2,1,0:T(8,128)} %absorb.1, f32[1024,128]{1,0:T(8,128)S(1)} %pad.16.clone.fsrc, f32[8,1024]{1,0:T(8,128)S(1)} %get-tuple-element.8.pattern, ...), custom_call_target="tpu_custom_call" | custom-call | flops 100663296 | bytes 14680064 | tf_op jit(solution)/shard_map/pallas_call | solution.py:421
  124.3 0.7 copy.16
  125.0 1.3 %copy.20 = f32[8,512,128]{2,1,0:T(8,128)} copy(f32[8,512,128]{2,1,0:T(8,128)S(1)} %get-tuple-element.16) | data formatting | bytes 4194304
  (5 shorter events, 0.1 us)
